TPU v7x, 32 devices: a whole 2x2x4 slice. The times are simulated.
32 devices in a mesh: prow: 4 (over x, core), pcol: 8 (over z, y).
Axes of the slice: x: 2, y: 2, z: 4, core: 2. Of those that a mesh axis runs over, the one named last changes fastest.
Arguments:
- blocks: bfloat16 [20480, 128, 128], P(('prow', 'pcol')), may hold values from -0.078125 to 0.078125
- row_index: int32 [20480], P(('prow', 'pcol')), may hold values from 0 to 511, as said below
- col_index: int32 [20480], P(('prow', 'pcol')), may hold values from 0 to 511, as said below
- send_tiles: int32 [512], P(('prow', 'pcol')), may hold values from 0 to 511, as said below
- lighting: bfloat16 [65536, 384], P(('prow', 'pcol')), may hold values from -6 to 6
- albedo: float32 [3, 65536], P(None, ('pcol', 'prow')), may hold values from 0.2 to 0.95
- emission: bfloat16 [65536, 384], P(('pcol', 'prow')), may hold values from -4 to 4
Outputs:
- radiance: bfloat16 [65536, 384], P(('pcol', 'prow'))
Inputs may be any that keep to these rules, and one draw needn't show every extreme that they name: `send_tiles`: group g (the blocks of device g) lists 16 distinct tiles in increasing order: exactly 4 from each of the 4 ranges of 16 block rows starting at c * 64 + r * 16, r = 0 .. 3, where c = g % 8. `row_index`: each block's row is one of its group's listed tiles, each listed tile has at least one block, and a group's blocks are ordered by row; counts per tile are uneven. `col_index`: the blocks of group g have columns in (g // 8) * 128 to (g // 8 + 1) * 128 - 1; a pair of row and column may repeat, and then the blocks add.
All inputs are finite; a program needn't handle non-finite values.
Results may differ from a plain program's by a relative error of at most 0.008.
Values may be sent and summed in bfloat16 or wider, within the bound.
A program may use at most 192 MiB of HBM per device.

v0:
```python
import functools

import jax
import jax.numpy as jnp
from jax import lax
from jax.experimental import pallas as pl
from jax.experimental.pallas import tpu as pltpu
from jax.sharding import PartitionSpec as P

GROUP = 8
BATCH = 8
MESH = pl.DeviceIdType.MESH


def ring_place(pcol, n):
    odd = pcol % 2
    return (1 - odd) * (pcol // 2) + odd * (n - 1 - pcol // 2)


def ring_device(place, n):
    late = place // (n // 2)
    return (1 - late) * (2 * place) + late * (2 * (n - 1 - place) + 1)


def fused(
    n,
    rows,
    colours,
    plan_ref,
    last_ref,
    col_ref,
    ids_ref,
    blocks_ref,
    light_ref,
    arr_ref,
    got_ref,
    *scratch,
):
    slabs = scratch[:colours]
    parts = scratch[colours : 2 * colours]
    blk, sums, ring_send, ring_recv, own_sem, blk_sem, ex_send, ex_recv, ex_own, id_send, id_recv, id_own = scratch[
        2 * colours :
    ]
    count = blocks_ref.shape[0]
    groups = plan_ref.shape[1]
    tiles = light_ref.shape[0]
    half = tiles // 2
    listed = last_ref.shape[0]
    per = listed // rows
    basis = slabs[0].shape[2]
    prow = lax.axis_index("prow")
    pcol = lax.axis_index("pcol")
    place = ring_place(pcol, n)
    after = ring_device((place + 1) % n, n)
    before = ring_device((place + n - 1) % n, n)
    messages = n - 1

    barrier = pltpu.get_barrier_semaphore()
    for side in (after, before):
        pl.semaphore_signal(barrier, inc=1, device_id={"pcol": side}, device_id_type=MESH)
    for d in range(1, rows):
        pl.semaphore_signal(barrier, inc=1, device_id={"prow": (prow + d) % rows}, device_id_type=MESH)

    own = [
        pltpu.make_async_copy(
            light_ref.at[:, :, pl.ds(c * basis, basis)], slabs[c].at[pl.ds(pcol * tiles, tiles)], own_sem.at[c]
        )
        for c in range(colours)
    ]
    for copy in own:
        copy.start()
    pl.semaphore_wait(barrier, 2 + rows - 1)

    def piece(c, m, way, arriving):
        step = m // 2
        part = (m + way) % 2
        if way == 0:
            source = (place + n - step - arriving) % n
        else:
            source = (place + step + arriving) % n
        at = ring_device(source, n) * tiles + part * half
        window = slabs[c].at[pl.ds(at, half)]
        return pltpu.make_async_remote_copy(
            src_ref=window,
            dst_ref=window,
            send_sem=ring_send.at[way, c, m],
            recv_sem=ring_recv.at[way, c, m],
            device_id={"pcol": before if way else after},
            device_id_type=MESH,
        )

    def to_row(c, d):
        target = (prow + d) % rows
        return pltpu.make_async_remote_copy(
            src_ref=parts[c].at[pl.ds(target * per, per)],
            dst_ref=arr_ref.at[c, prow],
            send_sem=ex_send.at[c, d],
            recv_sem=ex_recv.at[c, d],
            device_id={"prow": target},
            device_id_type=MESH,
        )

    def from_row(c, d):
        origin = (prow + rows - d) % rows
        return pltpu.make_async_remote_copy(
            src_ref=parts[c].at[pl.ds(0, per)],
            dst_ref=arr_ref.at[c, origin],
            send_sem=ex_send.at[c, d],
            recv_sem=ex_recv.at[c, d],
            device_id={"prow": origin},
            device_id_type=MESH,
        )

    def ids_to(d):
        target = (prow + d) % rows
        return pltpu.make_async_remote_copy(
            src_ref=ids_ref,
            dst_ref=got_ref.at[prow],
            send_sem=id_send.at[d],
            recv_sem=id_recv.at[d],
            device_id={"prow": target},
            device_id_type=MESH,
        )

    def ids_from(d):
        origin = (prow + rows - d) % rows
        return pltpu.make_async_remote_copy(
            src_ref=ids_ref,
            dst_ref=got_ref.at[origin],
            send_sem=id_send.at[d],
            recv_sem=id_recv.at[d],
            device_id={"prow": origin},
            device_id_type=MESH,
        )

    load = pltpu.make_async_copy(blocks_ref, blk.at[pl.ds(0, count)], blk_sem)

    def compute(c, low, high):
        def one(i, running):
            products = []
            for u in range(BATCH):
                base = plan_ref[0, i * BATCH + u]
                end = plan_ref[1, i * BATCH + u]
                left, right = [], []
                for j in range(GROUP):
                    at = base + j
                    inside = at < end
                    left.append(blk[jnp.where(inside, at, count)])
                    right.append(slabs[c][col_ref[jnp.where(inside, at, 0)]])
                products.append(
                    jnp.dot(
                        jnp.concatenate(left, axis=1),
                        jnp.concatenate(right, axis=0),
                        preferred_element_type=jnp.float32,
                    )
                )
            for u in range(BATCH):
                running = running * plan_ref[2, i * BATCH + u].astype(jnp.float32) + products[u]
                sums[i * BATCH + u + 1] = running
            return running

        lax.fori_loop(low, high, one, sums[low * BATCH])

    def exchange(c):
        for s in range(listed):
            parts[c][s] = sums[last_ref[s]].astype(jnp.bfloat16)
        for d in range(1, rows):
            to_row(c, d).start()
        pltpu.make_async_copy(parts[c].at[pl.ds(prow * per, per)], arr_ref.at[c, prow], ex_own.at[c]).start()

    def finish_ring(c):
        for m in range(max(messages - 2, 0), messages):
            for way in (0, 1):
                piece(c, m, way, 1).wait_recv()

    batches = groups // BATCH
    cuts = [batches * k // (messages - 1) for k in range(messages)]
    for c in range(colours):
        own[c].wait()
        for m in range(messages):
            for way in (0, 1):
                if m >= 2:
                    piece(c, m - 2, way, 1).wait_recv()
                piece(c, m, way, 0).start()
            if c == 0 and m == 1:
                load.start()
                blk[count] = jnp.zeros(blk.shape[1:], blk.dtype)
                sums[0] = jnp.zeros(sums.shape[1:], sums.dtype)
                for d in range(1, rows):
                    ids_to(d).start()
                pltpu.make_async_copy(ids_ref, got_ref.at[prow], id_own).start()
            if c >= 1 and m >= 1:
                if m == 1:
                    if c == 1:
                        load.wait()
                    finish_ring(c - 1)
                compute(c - 1, cuts[m - 1], cuts[m])
                if m == messages - 1:
                    exchange(c - 1)
    finish_ring(colours - 1)
    compute(colours - 1, 0, batches)
    exchange(colours - 1)
    for c in range(colours):
        for m in range(messages):
            for way in (0, 1):
                piece(c, m, way, 0).wait_send()
        for d in range(1, rows):
            to_row(c, d).wait_send()
            from_row(c, d).wait_recv()
        pltpu.make_async_copy(parts[c].at[pl.ds(prow * per, per)], arr_ref.at[c, prow], ex_own.at[c]).wait()
    for d in range(1, rows):
        ids_to(d).wait_send()
        ids_from(d).wait_recv()
    pltpu.make_async_copy(ids_ref, got_ref.at[prow], id_own).wait()


def finish(here_ref, arr_ref, albedo_ref, emission_ref, out_ref, total):
    rows, per = arr_ref.shape[1:3]
    step = pl.program_id(0)
    total[...] = jnp.zeros_like(total)
    for r in range(rows):
        for k in range(per):
            total[here_ref[r * per + k]] += arr_ref[0, r, k].astype(jnp.float32)
    for c in range(albedo_ref.shape[2]):

        @pl.when(step == c)
        def _():
            for t in range(total.shape[0]):
                lit = total[t] * albedo_ref[t][:, c : c + 1] + emission_ref[t].astype(jnp.float32)
                out_ref[t] = lit.astype(out_ref.dtype)


def per_device(blocks, row_index, col_index, send_tiles, lighting, albedo, emission):
    count, tile = blocks.shape[:2]
    width = lighting.shape[1]
    colours = albedo.shape[0]
    basis = width // colours
    listed = send_tiles.shape[0]
    rows = lax.axis_size("prow")
    n = lax.axis_size("pcol")
    tiles = lighting.shape[0] // tile
    owned = emission.shape[0] // tile
    per = listed // rows
    prow = lax.axis_index("prow")
    pcol = lax.axis_index("pcol")
    groups = (count + listed * (GROUP - 1)) // GROUP
    groups = -(-groups // BATCH) * BATCH

    first = jnp.sum((row_index[None, :] < send_tiles[:, None]).astype(jnp.int32), axis=1)
    past = jnp.sum((row_index[None, :] <= send_tiles[:, None]).astype(jnp.int32), axis=1)
    needed = (past - first + GROUP - 1) // GROUP
    order = jnp.arange(listed)
    ends = jnp.sum(jnp.where(order[None, :] <= order[:, None], needed[None, :], 0), axis=1)
    starts = ends - needed
    index = jnp.arange(groups)[:, None]
    inside = jnp.logical_and(index >= starts[None, :], index < ends[None, :])
    base = jnp.sum(jnp.where(inside, first[None, :] + (index - starts[None, :]) * GROUP, 0), axis=1)
    limit = jnp.sum(jnp.where(inside, past[None, :], 0), axis=1)
    keep = jnp.sum(jnp.where(jnp.logical_and(inside, index > starts[None, :]), 1, 0), axis=1)
    plan = jnp.stack([base, limit, keep])
    local_cols = col_index - prow * (n * tiles)
    ids = jnp.broadcast_to(jnp.pad(send_tiles, (0, 128 - listed))[None, :], (8, 128))

    half = tile * basis
    slab_bytes = n * tiles * half * 2 * colours
    vmem = (count + 1) * tile * tile * 2 + slab_bytes + (groups + 1) * half * 4 + colours * listed * half * 2
    smem = pl.BlockSpec(memory_space=pltpu.SMEM)
    hbm = pl.BlockSpec(memory_space=pl.ANY)
    arrived, got = pl.pallas_call(
        functools.partial(fused, n, rows, colours),
        out_shape=(
            jax.ShapeDtypeStruct((colours, rows, per, tile, basis), jnp.bfloat16),
            jax.ShapeDtypeStruct((rows, 8, 128), jnp.int32),
        ),
        in_specs=[smem, smem, smem, hbm, hbm, hbm],
        out_specs=(hbm, hbm),
        scratch_shapes=[pltpu.VMEM((n * tiles, tile, basis), jnp.bfloat16) for _ in range(colours)]
        + [pltpu.VMEM((listed, tile, basis), jnp.bfloat16) for _ in range(colours)]
        + [
            pltpu.VMEM((count + 1, tile, tile), jnp.bfloat16),
            pltpu.VMEM((groups + 1, tile, basis), jnp.float32),
            pltpu.SemaphoreType.DMA((2, colours, n - 1)),
            pltpu.SemaphoreType.DMA((2, colours, n - 1)),
            pltpu.SemaphoreType.DMA((colours,)),
            pltpu.SemaphoreType.DMA,
            pltpu.SemaphoreType.DMA((colours, rows)),
            pltpu.SemaphoreType.DMA((colours, rows)),
            pltpu.SemaphoreType.DMA((colours,)),
            pltpu.SemaphoreType.DMA((rows,)),
            pltpu.SemaphoreType.DMA((rows,)),
            pltpu.SemaphoreType.DMA,
        ],
        compiler_params=pltpu.CompilerParams(
            collective_id=0, has_side_effects=True, vmem_limit_bytes=max(vmem + (2 << 20), 58 << 20)
        ),
        cost_estimate=pl.CostEstimate(
            flops=2 * count * tile * tile * width, bytes_accessed=count * tile * tile * 2 + slab_bytes, transcendentals=0
        ),
    )(
        plan,
        ends,
        local_cols,
        ids,
        blocks,
        lighting.reshape(tiles, tile, width),
    )

    mine = lax.dynamic_slice_in_dim(got[:, 0, :], prow * per, per, axis=1)
    here = mine.reshape(-1) - (pcol * rows + prow) * owned
    out = pl.pallas_call(
        finish,
        out_shape=jax.ShapeDtypeStruct((owned, tile, width), jnp.bfloat16),
        grid=(colours,),
        in_specs=[
            smem,
            pl.BlockSpec((1, rows, per, tile, basis), lambda i: (i, 0, 0, 0, 0)),
            pl.BlockSpec((owned, tile, colours), lambda i: (0, 0, 0)),
            pl.BlockSpec((owned, tile, basis), lambda i: (0, 0, i)),
        ],
        out_specs=pl.BlockSpec((owned, tile, basis), lambda i: (0, 0, i)),
        scratch_shapes=[pltpu.VMEM((owned, tile, basis), jnp.float32)],
        compiler_params=pltpu.CompilerParams(vmem_limit_bytes=24 << 20),
    )(
        here,
        arrived,
        jnp.transpose(albedo).reshape(owned, tile, colours),
        emission.reshape(owned, tile, width),
    )
    return out.reshape(owned * tile, width)


def solution(mesh):
    placed = (
        P(("prow", "pcol"), None, None),
        P(("prow", "pcol")),
        P(("prow", "pcol")),
        P(("prow", "pcol")),
        P(("prow", "pcol"), None),
        P(None, ("pcol", "prow")),
        P(("pcol", "prow"), None),
    )
    return jax.shard_map(
        per_device, mesh=mesh, in_specs=placed, out_specs=P(("pcol", "prow"), None), check_vma=False
    )
```

profile of v0, /device:TPU:1, one launch (start us, length us, event | category | flops | bytes accessed | tf_op | source)
XLA Modules:
  0.0 151.0 jit_solution(3707248376778271251)
XLA Ops:
  0.0 0.7 pad.4
  0.7 0.9 convert_reduce_fusion
  1.6 0.1 select_reduce_fusion.3.last_ref
  1.7 0.0 copy-start.2
  1.7 0.1 select_reduce_fusion.2
  1.8 0.6 pad_add_fusion.plan_ref
  2.4 0.6 broadcast_in_dim.39.ids_ref
  3.0 1.3 broadcast_subtract_fusion.col_ref
  4.2 1.1 copy.9
  5.4 0.0 copy-done.2
  5.4 0.0 copy-start
  5.4 140.0 %shard_map.73 = (bf16[3,4,4,128,128]{4,3,2,1,0:T(8,128)(2,1)}, s32[4,8,128]{2,1,0:T(8,128)}) custom-call(s32[3,96]{1,0:T(4,128)} %pad_add_fusion.plan_ref, s32[16]{0:T(128)} %copy-done.2, s32[640]{0:T(1024)} %broadcast_subtract_fusion.col_ref, s32[8,128]{1,0:T(8,128)} %broadcast_in_dim.39.ids_ref, bf16[640,128,128]{2,1,0:T(8,128)(2,1)} %blocks_ref.1, ...), custom_call_target="tpu_custom_call" | custom-call | flops 8053063680 | bytes 33554432 | tf_op jit(solution)/shard_map/pallas_call | solution.py:269
  145.4 0.7 slice.3
  146.1 0.1 subtract_reduce_fusion
  146.2 0.1 sub.59.here_ref
  146.3 0.0 copy-done
  146.3 0.0 copy-start.1
  146.3 1.4 copy-done.1
  147.7 3.3 %shard_map.74 = bf16[16,128,384]{2,1,0:T(8,128)(2,1)} custom-call(s32[16]{0:T(128)S(1)} %sub.59.here_ref, bf16[3,4,4,128,128]{4,3,2,1,0:T(8,128)(2,1)S(1)} %copy-done.1, f32[16,128,3]{2,1,0:T(8,128)S(1)} %bitcast.8, bf16[16,128,384]{2,1,0:T(8,128)(2,1)S(1)} %bitcast.9), custom_call_target="tpu_custom_call" | custom-call | tf_op jit(solution)/shard_map/pallas_call | solution.py:310
  (2 shorter events, 0.0 us)
Async XLA Ops:
  1.7 3.7 %copy-start.2 = (s32[16]{0:T(128)}, s32[16]{0:T(128)S(1)}, u32[]{:S(2)}) copy-start(s32[16]{0:T(128)S(1)} %select_reduce_fusion.3.last_ref) | copy-start | bytes 196
  5.4 140.9 %copy-start = (bf16[2048,384]{1,0:T(8,128)(2,1)S(1)}, bf16[2048,384]{1,0:T(8,128)(2,1)}, u32[]{:S(2)}) copy-start(bf16[2048,384]{1,0:T(8,128)(2,1)} %param.13) | copy-start | bytes 4718596
  146.3 1.4 copy-start.1
where the time goes:
time: 151 us
  Pallas kernels  143 us (95%)
  local copies, waits for them, and re-layouts  4.59 us (3%)
  other arithmetic  3.05 us (2%)
    pallas_call x1, Pallas kernels, per_device(): pl.pallas_call(functools.partial(fused, n, rows, colours), out_shape=(jax...  140 us
    pallas_call x1, Pallas kernels, per_device(): pl.pallas_call(finish, out_shape=jax.ShapeDtypeStruct((owned, tile, width...  3.33 us

commit v1 on v0

v1 whole, which is shorter than its diff:
```python
import functools

import jax
import jax.numpy as jnp
from jax import lax
from jax.experimental import pallas as pl
from jax.experimental.pallas import tpu as pltpu
from jax.sharding import PartitionSpec as P

GROUP = 8
BATCH = 12
LATE = 32
MESH = pl.DeviceIdType.MESH


def ring_place(pcol, n):
    odd = pcol % 2
    return (1 - odd) * (pcol // 2) + odd * (n - 1 - pcol // 2)


def ring_device(place, n):
    late = place // (n // 2)
    return (1 - late) * (2 * place) + late * (2 * (n - 1 - place) + 1)


def chunks_of(colours, tile):
    whole = [(c, 0, tile) for c in range(colours - 1)]
    return whole + [(colours - 1, 0, tile - LATE), (colours - 1, tile - LATE, LATE)]


def fused(
    n,
    rows,
    colours,
    groups,
    row_ref,
    col_ref,
    send_ref,
    blocks_ref,
    light_ref,
    albedo_ref,
    emission_ref,
    out_ref,
    *scratch,
):
    count, tile = blocks_ref.shape[:2]
    tiles = light_ref.shape[0]
    owned = emission_ref.shape[0]
    chunks = chunks_of(colours, tile)
    take = iter(scratch)
    slabs = [next(take) for _ in chunks]
    arrived = [next(take) for _ in range(colours)]
    lit = [next(take) for _ in range(colours)]
    parts = [next(take) for _ in range(2)]
    got = [next(take) for _ in range(rows)]
    (
        blk,
        packed,
        sums,
        alb_in,
        alb_rows,
        alb_cols,
        row_s,
        col_s,
        past_s,
        last_s,
        gsrc,
        gcol,
        keep_s,
        pos_s,
        ring_send,
        ring_recv,
        own_sem,
        blk_sem,
        index_sem,
        alb_sem,
        em_sem,
        out_sem,
        ex_send,
        ex_recv,
        ex_own,
        id_send,
        id_recv,
    ) = take
    half = tiles // 2
    listed = send_ref.shape[0]
    per = listed // rows
    basis = slabs[0].shape[2]
    batches = groups // BATCH
    prow = lax.axis_index("prow")
    pcol = lax.axis_index("pcol")
    place = ring_place(pcol, n)
    after = ring_device((place + 1) % n, n)
    before = ring_device((place + n - 1) % n, n)
    messages = n - 1

    barrier = pltpu.get_barrier_semaphore()
    for side in (after, before):
        pl.semaphore_signal(barrier, inc=1, device_id={"pcol": side}, device_id_type=MESH)
    for d in range(1, rows):
        pl.semaphore_signal(barrier, inc=1, device_id={"prow": (prow + d) % rows}, device_id_type=MESH)

    own = [
        pltpu.make_async_copy(
            light_ref.at[:, pl.ds(o, h), pl.ds(c * basis, basis)], slabs[k].at[pl.ds(pcol * tiles, tiles)], own_sem.at[k]
        )
        for k, (c, o, h) in enumerate(chunks)
    ]
    for copy in own:
        copy.start()
    loads = [
        pltpu.make_async_copy(row_ref, row_s, index_sem.at[0]),
        pltpu.make_async_copy(col_ref, col_s, index_sem.at[1]),
        pltpu.make_async_copy(send_ref, got[0], index_sem.at[2]),
    ]
    load = pltpu.make_async_copy(blocks_ref, blk.at[pl.ds(0, count)], blk_sem)
    load_albedo = pltpu.make_async_copy(albedo_ref, alb_in, alb_sem)
    load_emission = [
        pltpu.make_async_copy(emission_ref.at[:, :, pl.ds(c * basis, basis)], lit[c], em_sem.at[c]) for c in range(colours)
    ]
    store_out = [
        pltpu.make_async_copy(lit[c], out_ref.at[:, :, pl.ds(c * basis, basis)], out_sem.at[c]) for c in range(colours)
    ]
    pl.semaphore_wait(barrier, 2 + rows - 1)

    def piece(k, m, way, arriving):
        step = m // 2
        part = (m + way) % 2
        if way == 0:
            source = (place + n - step - arriving) % n
        else:
            source = (place + step + arriving) % n
        at = ring_device(source, n) * tiles + part * half
        window = slabs[k].at[pl.ds(at, half)]
        return pltpu.make_async_remote_copy(
            src_ref=window,
            dst_ref=window,
            send_sem=ring_send.at[way, k, m],
            recv_sem=ring_recv.at[way, k, m],
            device_id={"pcol": before if way else after},
            device_id_type=MESH,
        )

    def to_row(c, d):
        target = (prow + d) % rows
        return pltpu.make_async_remote_copy(
            src_ref=parts[c % 2].at[pl.ds(target * per, per)],
            dst_ref=arrived[c].at[pl.ds(prow * per, per)],
            send_sem=ex_send.at[c, d],
            recv_sem=ex_recv.at[c, d],
            device_id={"prow": target},
            device_id_type=MESH,
        )

    def from_row(c, d):
        origin = (prow + rows - d) % rows
        return pltpu.make_async_remote_copy(
            src_ref=parts[c % 2].at[pl.ds(0, per)],
            dst_ref=arrived[c].at[pl.ds(origin * per, per)],
            send_sem=ex_send.at[c, d],
            recv_sem=ex_recv.at[c, d],
            device_id={"prow": origin},
            device_id_type=MESH,
        )

    def stay(c):
        return pltpu.make_async_copy(
            parts[c % 2].at[pl.ds(prow * per, per)], arrived[c].at[pl.ds(prow * per, per)], ex_own.at[c]
        )

    def ids(d):
        return pltpu.make_async_remote_copy(
            src_ref=send_ref,
            dst_ref=got[d],
            send_sem=id_send.at[d],
            recv_sem=id_recv.at[d],
            device_id={"prow": (prow + d) % rows},
            device_id_type=MESH,
        )

    def start_loads():
        for copy in loads:
            copy.start()
        for d in range(1, rows):
            ids(d).start()
        load.start()
        load_albedo.start()
        for copy in load_emission:
            copy.start()

    def make_plan():
        for copy in loads:
            copy.wait()

        def slot(s, carry):
            first, end = carry
            wanted = got[0][s]

            def narrow(_, bounds):
                low, high = bounds
                middle = (low + high) // 2
                up = jnp.logical_and(low < high, row_s[jnp.minimum(middle, count - 1)] <= wanted)
                return jnp.where(up, middle + 1, low), jnp.where(up, high, middle)

            past, _ = lax.fori_loop(0, count.bit_length(), narrow, (first, jnp.int32(count)))
            end = end + (past - first + GROUP - 1) // GROUP
            past_s[s] = past
            last_s[s] = jnp.clip(end - 1, 0, groups - 1)
            return past, end

        lax.fori_loop(0, listed, slot, (jnp.int32(0), jnp.int32(0)))
        low_col = prow * (n * tiles)

        def group(i, carry):
            s, at, keep = carry
            end = past_s[jnp.minimum(s, listed - 1)]
            for j in range(GROUP):
                inside = at + j < end
                gsrc[i * GROUP + j] = jnp.where(inside, at + j, count)
                column = col_s[jnp.minimum(at + j, count - 1)] - low_col
                gcol[i * GROUP + j] = jnp.where(inside, jnp.clip(column, 0, n * tiles - 1), 0)
            keep_s[i] = keep
            done = at + GROUP >= end
            return (
                jnp.where(done, s + 1, s),
                jnp.minimum(at + GROUP, end),
                jnp.where(done, 0, 1),
            )

        lax.fori_loop(0, groups, group, (jnp.int32(0), jnp.int32(0), jnp.int32(0)))

    def make_places():
        for d in range(1, rows):
            ids(d).wait_send()
            ids(d).wait_recv()
        low_tile = (pcol * rows + prow) * owned

        def place_of(t, carry):
            for d in range(rows):
                origin = (prow + rows - d) % rows
                at = jnp.int32(listed)
                for k in range(per):
                    at = jnp.where(got[d][prow * per + k] == low_tile + t, origin * per + k, at)
                pos_s[t * rows + d] = at
            return carry

        lax.fori_loop(0, owned, place_of, jnp.int32(0))

    def make_albedo():
        load_albedo.wait()
        alb_rows[...] = jnp.zeros(alb_rows.shape, alb_rows.dtype)
        for c in range(colours):
            for t in range(owned):
                alb_rows[pl.ds(c * owned + t, 1), :] = alb_in[pl.ds(c, 1), pl.ds(t * tile, tile)]
        alb_cols[...] = jnp.transpose(alb_rows[...])

    def pack():
        each = tile // LATE
        lane = lax.broadcasted_iota(jnp.int32, (tile, tile), 1)

        def one(g, carry):
            for h in range(GROUP // each):
                joined = jnp.zeros((tile, tile), blk.dtype)
                for j in range(each):
                    block = blk[gsrc[g * GROUP + h * each + j]]
                    shift = (j * LATE + LATE) % tile
                    if shift:
                        block = jnp.concatenate([block[:, tile - shift :], block[:, : tile - shift]], axis=1)
                    mine = jnp.logical_and(lane >= j * LATE, lane < (j + 1) * LATE)
                    joined = jnp.where(mine, block, joined)
                packed[g, :, pl.ds(h * tile, tile)] = joined
            return carry

        lax.fori_loop(0, groups, one, jnp.int32(0))

    def full_operands(k, g):
        left, right = [], []
        for j in range(GROUP):
            left.append(blk[gsrc[g * GROUP + j]])
            lighting = slabs[k][gcol[g * GROUP + j]]
            if lighting.shape[0] < tile:
                fill = jnp.zeros((tile - lighting.shape[0], basis), lighting.dtype)
                lighting = jnp.concatenate([lighting, fill], axis=0)
            right.append(lighting)
        return jnp.concatenate(left, axis=1), jnp.concatenate(right, axis=0)

    def late_operands(k, g):
        right = [slabs[k][gcol[g * GROUP + j]] for j in range(GROUP)]
        return packed[g], jnp.concatenate(right, axis=0)

    def compute(operands, k, low, high, running):
        def one(i, running):
            products = []
            for u in range(BATCH):
                left, right = operands(k, i * BATCH + u)
                products.append(jnp.dot(left, right, preferred_element_type=jnp.float32))
            for u in range(BATCH):
                running = running * keep_s[i * BATCH + u].astype(jnp.float32) + products[u]
                sums[i * BATCH + u] = running.astype(sums.dtype)
            return running

        return lax.fori_loop(low, high, one, running)

    def collect(c, send, add):
        for d in list(range(rows // 2, rows)) + list(range(rows // 2)):
            target = (prow + d) % rows
            for j in range(per):
                s = target * per + j
                value = sums[last_s[s]]
                if add:
                    value = (parts[c % 2][s].astype(jnp.float32) + value.astype(jnp.float32)).astype(sums.dtype)
                parts[c % 2][s] = value
            if send:
                if d:
                    to_row(c, d).start()
                else:
                    stay(c).start()

    def finish(c):
        for d in range(1, rows):
            to_row(c, d).wait_send()
            from_row(c, d).wait_recv()
        stay(c).wait()
        load_emission[c].wait()
        for t in range(owned):
            total = arrived[c][pos_s[t * rows]].astype(jnp.float32)
            for d in range(1, rows):
                total = total + arrived[c][pos_s[t * rows + d]].astype(jnp.float32)
            scale = alb_cols[:, pl.ds(c * owned + t, 1)]
            lit[c][t] = (total * scale + lit[c][t].astype(jnp.float32)).astype(lit[c].dtype)
        store_out[c].start()

    final = len(chunks) - 1
    steps = min(messages - 1, batches)
    cuts = [batches * i // steps for i in range(steps + 1)]
    for k in range(len(chunks)):
        own[k].wait()
        running = jnp.zeros((tile, basis), jnp.float32)
        for m in range(messages):
            for way in (0, 1):
                if m >= 2:
                    piece(k, m - 2, way, 1).wait_recv()
                piece(k, m, way, 0).start()
            if k == 0:
                if m == 1:
                    start_loads()
                    blk[count] = jnp.zeros(blk.shape[1:], blk.dtype)
                    for c in range(colours):
                        arrived[c][listed] = jnp.zeros(arrived[c].shape[1:], arrived[c].dtype)
                    make_plan()
                if m == 2:
                    make_places()
                    make_albedo()
                if m == 3:
                    load.wait()
                    pack()
            elif m >= 1:
                if m == 1:
                    for last in range(max(messages - 2, 0), messages):
                        for way in (0, 1):
                            piece(k - 1, last, way, 1).wait_recv()
                if m <= steps:
                    running = compute(full_operands, k - 1, cuts[m - 1], cuts[m], running)
                if m == steps:
                    collect(chunks[k - 1][0], k < final, False)
                if m == max(steps - 1, 1) and k >= 2:
                    finish(k - 2)
    for m in range(messages):
        for k in range(final):
            for way in (0, 1):
                piece(k, m, way, 0).wait_send()
    for m in range(max(messages - 2, 0), messages):
        for way in (0, 1):
            piece(final, m, way, 1).wait_recv()
    compute(late_operands, final, 0, batches, jnp.zeros((tile, basis), jnp.float32))
    collect(colours - 1, True, True)
    for m in range(messages):
        for way in (0, 1):
            piece(final, m, way, 0).wait_send()
    finish(colours - 1)
    for c in range(colours):
        store_out[c].wait()


def per_device(blocks, row_index, col_index, send_tiles, lighting, albedo, emission):
    count, tile = blocks.shape[:2]
    width = lighting.shape[1]
    colours = albedo.shape[0]
    basis = width // colours
    listed = send_tiles.shape[0]
    rows = lax.axis_size("prow")
    n = lax.axis_size("pcol")
    tiles = lighting.shape[0] // tile
    owned = emission.shape[0] // tile
    groups = (count + listed * (GROUP - 1)) // GROUP
    groups = -(-groups // BATCH) * BATCH
    chunks = chunks_of(colours, tile)
    final = len(chunks)

    hbm = pl.BlockSpec(memory_space=pl.ANY)
    bf16, f32, i32 = jnp.bfloat16, jnp.float32, jnp.int32
    dma = pltpu.SemaphoreType.DMA
    scratch = [pltpu.VMEM((n * tiles, h, basis), bf16) for _, _, h in chunks]
    scratch += [pltpu.VMEM((listed + 1, tile, basis), bf16) for _ in range(colours)]
    scratch += [pltpu.VMEM((owned, tile, basis), bf16) for _ in range(colours)]
    scratch += [pltpu.VMEM((listed, tile, basis), bf16) for _ in range(2)]
    scratch += [pltpu.SMEM((listed,), i32) for _ in range(rows)]
    scratch += [
        pltpu.VMEM((count + 1, tile, tile), bf16),
        pltpu.VMEM((groups, tile, GROUP * LATE), bf16),
        pltpu.VMEM((groups, tile, basis), bf16),
        pltpu.VMEM((colours, owned * tile), f32),
        pltpu.VMEM((tile, tile), f32),
        pltpu.VMEM((tile, tile), f32),
        pltpu.SMEM((count,), i32),
        pltpu.SMEM((count,), i32),
        pltpu.SMEM((listed,), i32),
        pltpu.SMEM((listed,), i32),
        pltpu.SMEM((groups * GROUP,), i32),
        pltpu.SMEM((groups * GROUP,), i32),
        pltpu.SMEM((groups,), i32),
        pltpu.SMEM((owned * rows,), i32),
        dma((2, final, n - 1)),
        dma((2, final, n - 1)),
        dma((final,)),
        dma,
        dma((3,)),
        dma,
        dma((colours,)),
        dma((colours,)),
        dma((colours, rows)),
        dma((colours, rows)),
        dma((colours,)),
        dma((rows,)),
        dma((rows,)),
    ]
    tile_bytes = tile * basis * 2
    vmem = (count + 1) * tile * tile * 2 + groups * tile * (GROUP * LATE + basis) * 2
    vmem += (n * tiles * colours + (listed + 1 + owned) * colours + 2 * listed) * tile_bytes
    out = pl.pallas_call(
        functools.partial(fused, n, rows, colours, groups),
        out_shape=jax.ShapeDtypeStruct((owned, tile, width), bf16),
        in_specs=[hbm] * 7,
        out_specs=hbm,
        scratch_shapes=scratch,
        compiler_params=pltpu.CompilerParams(
            collective_id=0, has_side_effects=True, vmem_limit_bytes=max(vmem + (2 << 20), 58 << 20)
        ),
        cost_estimate=pl.CostEstimate(
            flops=2 * count * tile * tile * width,
            bytes_accessed=count * tile * tile * 2 + n * tiles * colours * tile_bytes,
            transcendentals=0,
        ),
    )(
        row_index,
        col_index,
        send_tiles,
        blocks,
        lighting.reshape(tiles, tile, width),
        albedo,
        emission.reshape(owned, tile, width),
    )
    return out.reshape(owned * tile, width)


def solution(mesh):
    placed = (
        P(("prow", "pcol"), None, None),
        P(("prow", "pcol")),
        P(("prow", "pcol")),
        P(("prow", "pcol")),
        P(("prow", "pcol"), None),
        P(None, ("pcol", "prow")),
        P(("pcol", "prow"), None),
    )
    return jax.shard_map(
        per_device, mesh=mesh, in_specs=placed, out_specs=P(("pcol", "prow"), None), check_vma=False
    )
```

time: 151 us -> 143 us (0.947)
  other arithmetic: 3.05 us -> 0 us
  Pallas kernels: 143 us -> 140 us
  local copies, waits for them, and re-layouts: 4.59 us -> 2.71 us
    pallas_call x2 -> x1, Pallas kernels: 143 us -> 140 us  [per_device(): pl.pallas_call(functools.partial(fused, n, rows, colours, groups), out_sh...]
where the time goes in v1:
time: 143 us
  Pallas kernels  140 us (98%)
  local copies, waits for them, and re-layouts  2.71 us (2%)
    pallas_call x1, Pallas kernels, per_device(): pl.pallas_call(functools.partial(fused, n, rows, colours, groups), out_sh...  140 us

profile of v1, /device:TPU:1, one launch (start us, length us, event | category | flops | bytes accessed | tf_op | source)
XLA Modules:
  0.0 142.9 jit_solution(15010063808766339821)
XLA Ops:
  0.0 140.1 %shard_map.73 = bf16[16,128,384]{2,1,0:T(8,128)(2,1)} custom-call(s32[640]{0:T(1024)} %row_ref.1, s32[640]{0:T(1024)} %col_ref.1, s32[16]{0:T(128)} %send_ref.1, bf16[640,128,128]{2,1,0:T(8,128)(2,1)} %blocks_ref.1, bf16[16,128,384]{2,1,0:T(8,128)(2,1)} %bitcast.4, f32[3,2048]{1,0:T(4,128)} %albedo_ref.1, bf16[16,128,384]{2,1,0:T(8,128)(2,1)} %bitcast.5), custom_call_target="tpu_custom_call" | custom-call | flops 8053063680 | bytes 33554432 | tf_op jit(solution)/shard_map/pallas_call | solution.py:440
  140.2 2.7 %copy.9 = bf16[2048,384]{1,0:T(8,128)(2,1)} copy(bf16[2048,384]{1,0:T(8,128)(2,1)} %bitcast.3) | data formatting | bytes 3145728

commit v2 on v1

--- a/solution.py
+++ b/solution.py
@@ -9,7 +9,7 @@
 
 GROUP = 8
 BATCH = 12
-LATE = 32
+MIB = 1 << 20
 MESH = pl.DeviceIdType.MESH
 
 
@@ -23,9 +23,14 @@
     return (1 - late) * (2 * place) + late * (2 * (n - 1 - place) + 1)
 
 
-def chunks_of(colours, tile):
+def chunks_of(colours, tile, late):
     whole = [(c, 0, tile) for c in range(colours - 1)]
-    return whole + [(colours - 1, 0, tile - LATE), (colours - 1, tile - LATE, LATE)]
+    return whole + [(colours - 1, 0, tile - late), (colours - 1, tile - late, late)]
+
+
+def units_of(colours, tile):
+    whole = [(c, 0, tile) for c in range(colours - 1)]
+    return whole + [(colours - 1, 0, tile // 2), (colours - 1, tile // 2, tile // 2)]
 
 
 def fused(
@@ -33,6 +38,7 @@
     rows,
     colours,
     groups,
+    late,
     row_ref,
     col_ref,
     send_ref,
@@ -46,10 +52,11 @@
     count, tile = blocks_ref.shape[:2]
     tiles = light_ref.shape[0]
     owned = emission_ref.shape[0]
-    chunks = chunks_of(colours, tile)
+    chunks = chunks_of(colours, tile, late)
+    units = units_of(colours, tile)
     take = iter(scratch)
     slabs = [next(take) for _ in chunks]
-    arrived = [next(take) for _ in range(colours)]
+    arrived = [next(take) for _ in units]
     lit = [next(take) for _ in range(colours)]
     parts = [next(take) for _ in range(2)]
     got = [next(take) for _ in range(rows)]
@@ -119,7 +126,10 @@
         pltpu.make_async_copy(emission_ref.at[:, :, pl.ds(c * basis, basis)], lit[c], em_sem.at[c]) for c in range(colours)
     ]
     store_out = [
-        pltpu.make_async_copy(lit[c], out_ref.at[:, :, pl.ds(c * basis, basis)], out_sem.at[c]) for c in range(colours)
+        pltpu.make_async_copy(
+            lit[c].at[:, pl.ds(o, h)], out_ref.at[:, pl.ds(o, h), pl.ds(c * basis, basis)], out_sem.at[u]
+        )
+        for u, (c, o, h) in enumerate(units)
     ]
     pl.semaphore_wait(barrier, 2 + rows - 1)
 
@@ -141,31 +151,34 @@
             device_id_type=MESH,
         )
 
-    def to_row(c, d):
+    def to_row(u, d):
+        c, o, h = units[u]
         target = (prow + d) % rows
         return pltpu.make_async_remote_copy(
-            src_ref=parts[c % 2].at[pl.ds(target * per, per)],
-            dst_ref=arrived[c].at[pl.ds(prow * per, per)],
-            send_sem=ex_send.at[c, d],
-            recv_sem=ex_recv.at[c, d],
+            src_ref=parts[c % 2].at[pl.ds(target * per, per), pl.ds(o, h)],
+            dst_ref=arrived[u].at[pl.ds(prow * per, per)],
+            send_sem=ex_send.at[u, d],
+            recv_sem=ex_recv.at[u, d],
             device_id={"prow": target},
             device_id_type=MESH,
         )
 
-    def from_row(c, d):
+    def from_row(u, d):
+        c, o, h = units[u]
         origin = (prow + rows - d) % rows
         return pltpu.make_async_remote_copy(
-            src_ref=parts[c % 2].at[pl.ds(0, per)],
-            dst_ref=arrived[c].at[pl.ds(origin * per, per)],
-            send_sem=ex_send.at[c, d],
-            recv_sem=ex_recv.at[c, d],
+            src_ref=parts[c % 2].at[pl.ds(0, per), pl.ds(o, h)],
+            dst_ref=arrived[u].at[pl.ds(origin * per, per)],
+            send_sem=ex_send.at[u, d],
+            recv_sem=ex_recv.at[u, d],
             device_id={"prow": origin},
             device_id_type=MESH,
         )
 
-    def stay(c):
+    def stay(u):
+        c, o, h = units[u]
         return pltpu.make_async_copy(
-            parts[c % 2].at[pl.ds(prow * per, per)], arrived[c].at[pl.ds(prow * per, per)], ex_own.at[c]
+            parts[c % 2].at[pl.ds(prow * per, per), pl.ds(o, h)], arrived[u].at[pl.ds(prow * per, per)], ex_own.at[u]
         )
 
     def ids(d):
@@ -254,8 +267,8 @@
                 alb_rows[pl.ds(c * owned + t, 1), :] = alb_in[pl.ds(c, 1), pl.ds(t * tile, tile)]
         alb_cols[...] = jnp.transpose(alb_rows[...])
 
-    def pack():
-        each = tile // LATE
+    def pack(low, high):
+        each = tile // late
         lane = lax.broadcasted_iota(jnp.int32, (tile, tile), 1)
 
         def one(g, carry):
@@ -263,15 +276,15 @@
                 joined = jnp.zeros((tile, tile), blk.dtype)
                 for j in range(each):
                     block = blk[gsrc[g * GROUP + h * each + j]]
-                    shift = (j * LATE + LATE) % tile
+                    shift = (j * late + late) % tile
                     if shift:
                         block = jnp.concatenate([block[:, tile - shift :], block[:, : tile - shift]], axis=1)
-                    mine = jnp.logical_and(lane >= j * LATE, lane < (j + 1) * LATE)
+                    mine = jnp.logical_and(lane >= j * late, lane < (j + 1) * late)
                     joined = jnp.where(mine, block, joined)
                 packed[g, :, pl.ds(h * tile, tile)] = joined
             return carry
 
-        lax.fori_loop(0, groups, one, jnp.int32(0))
+        lax.fori_loop(low, high, one, jnp.int32(0))
 
     def full_operands(k, g):
         left, right = [], []
@@ -284,55 +297,60 @@
             right.append(lighting)
         return jnp.concatenate(left, axis=1), jnp.concatenate(right, axis=0)
 
-    def late_operands(k, g):
+    def late_operands(k, g, o, h):
         right = [slabs[k][gcol[g * GROUP + j]] for j in range(GROUP)]
-        return packed[g], jnp.concatenate(right, axis=0)
-
-    def compute(operands, k, low, high, running):
+        return packed[g, pl.ds(o, h)], jnp.concatenate(right, axis=0)
+
+    def compute(operands, batch, o, h, low, high, running):
         def one(i, running):
             products = []
-            for u in range(BATCH):
-                left, right = operands(k, i * BATCH + u)
+            for b in range(batch):
+                left, right = operands(i * batch + b)
                 products.append(jnp.dot(left, right, preferred_element_type=jnp.float32))
-            for u in range(BATCH):
-                running = running * keep_s[i * BATCH + u].astype(jnp.float32) + products[u]
-                sums[i * BATCH + u] = running.astype(sums.dtype)
+            for b in range(batch):
+                running = running * keep_s[i * batch + b].astype(jnp.float32) + products[b]
+                sums[i * batch + b, pl.ds(o, h)] = running.astype(sums.dtype)
             return running
 
         return lax.fori_loop(low, high, one, running)
 
-    def collect(c, send, add):
+    def collect(c, o, h, add, u):
         for d in list(range(rows // 2, rows)) + list(range(rows // 2)):
             target = (prow + d) % rows
             for j in range(per):
                 s = target * per + j
-                value = sums[last_s[s]]
+                value = sums[last_s[s], pl.ds(o, h)]
                 if add:
-                    value = (parts[c % 2][s].astype(jnp.float32) + value.astype(jnp.float32)).astype(sums.dtype)
-                parts[c % 2][s] = value
-            if send:
+                    before = parts[c % 2][s, pl.ds(o, h)]
+                    value = (before.astype(jnp.float32) + value.astype(jnp.float32)).astype(sums.dtype)
+                parts[c % 2][s, pl.ds(o, h)] = value
+            if u is not None:
                 if d:
-                    to_row(c, d).start()
+                    to_row(u, d).start()
                 else:
-                    stay(c).start()
-
-    def finish(c):
+                    stay(u).start()
+
+    def finish(u):
+        c, o, h = units[u]
         for d in range(1, rows):
-            to_row(c, d).wait_send()
-            from_row(c, d).wait_recv()
-        stay(c).wait()
-        load_emission[c].wait()
+            to_row(u, d).wait_send()
+            from_row(u, d).wait_recv()
+        stay(u).wait()
+        if o == 0:
+            load_emission[c].wait()
         for t in range(owned):
-            total = arrived[c][pos_s[t * rows]].astype(jnp.float32)
+            total = arrived[u][pos_s[t * rows]].astype(jnp.float32)
             for d in range(1, rows):
-                total = total + arrived[c][pos_s[t * rows + d]].astype(jnp.float32)
-            scale = alb_cols[:, pl.ds(c * owned + t, 1)]
-            lit[c][t] = (total * scale + lit[c][t].astype(jnp.float32)).astype(lit[c].dtype)
-        store_out[c].start()
+                total = total + arrived[u][pos_s[t * rows + d]].astype(jnp.float32)
+            scale = alb_cols[pl.ds(o, h), pl.ds(c * owned + t, 1)]
+            before = lit[c][t, pl.ds(o, h)].astype(jnp.float32)
+            lit[c][t, pl.ds(o, h)] = (total * scale + before).astype(lit[c].dtype)
+        store_out[u].start()
 
     final = len(chunks) - 1
     steps = min(messages - 1, batches)
     cuts = [batches * i // steps for i in range(steps + 1)]
+    packs = [groups * i // (messages - 3) for i in range(messages - 2)]
     for k in range(len(chunks)):
         own[k].wait()
         running = jnp.zeros((tile, basis), jnp.float32)
@@ -345,41 +363,48 @@
                 if m == 1:
                     start_loads()
                     blk[count] = jnp.zeros(blk.shape[1:], blk.dtype)
-                    for c in range(colours):
-                        arrived[c][listed] = jnp.zeros(arrived[c].shape[1:], arrived[c].dtype)
+                    for buffer in arrived:
+                        buffer[listed] = jnp.zeros(buffer.shape[1:], buffer.dtype)
                     make_plan()
                 if m == 2:
                     make_places()
                     make_albedo()
                 if m == 3:
                     load.wait()
-                    pack()
+                if m >= 3:
+                    pack(packs[m - 3], packs[m - 2])
             elif m >= 1:
                 if m == 1:
                     for last in range(max(messages - 2, 0), messages):
                         for way in (0, 1):
                             piece(k - 1, last, way, 1).wait_recv()
                 if m <= steps:
-                    running = compute(full_operands, k - 1, cuts[m - 1], cuts[m], running)
+                    operands = functools.partial(full_operands, k - 1)
+                    running = compute(operands, BATCH, 0, tile, cuts[m - 1], cuts[m], running)
                 if m == steps:
-                    collect(chunks[k - 1][0], k < final, False)
+                    collect(chunks[k - 1][0], 0, tile, False, k - 1 if k < final else None)
                 if m == max(steps - 1, 1) and k >= 2:
                     finish(k - 2)
-    for m in range(messages):
-        for k in range(final):
-            for way in (0, 1):
-                piece(k, m, way, 0).wait_send()
+                for way in (0, 1):
+                    piece(k - 1, m, way, 0).wait_send()
+                    if m == 1:
+                        piece(k - 1, 0, way, 0).wait_send()
     for m in range(max(messages - 2, 0), messages):
         for way in (0, 1):
             piece(final, m, way, 1).wait_recv()
-    compute(late_operands, final, 0, batches, jnp.zeros((tile, basis), jnp.float32))
-    collect(colours - 1, True, True)
+    batch = 2 * BATCH if batches % 2 == 0 else BATCH
+    for u in range(colours - 1, len(units)):
+        c, o, h = units[u]
+        operands = functools.partial(late_operands, final, o=o, h=h)
+        compute(operands, batch, o, h, 0, groups // batch, jnp.zeros((h, basis), jnp.float32))
+        collect(c, o, h, True, u)
     for m in range(messages):
         for way in (0, 1):
             piece(final, m, way, 0).wait_send()
-    finish(colours - 1)
-    for c in range(colours):
-        store_out[c].wait()
+    for u in range(colours - 1, len(units)):
+        finish(u)
+    for copy in store_out:
+        copy.wait()
 
 
 def per_device(blocks, row_index, col_index, send_tiles, lighting, albedo, emission):
@@ -394,20 +419,27 @@
     owned = emission.shape[0] // tile
     groups = (count + listed * (GROUP - 1)) // GROUP
     groups = -(-groups // BATCH) * BATCH
-    chunks = chunks_of(colours, tile)
+    units = units_of(colours, tile)
+
+    def vmem_of(late):
+        tall = n * tiles * colours + (listed + 1 + owned) * colours + 2 * listed + groups
+        return ((count + 1) * tile * tile + groups * tile * GROUP * late + tall * tile * basis) * 2
+
+    late = tile // 2 if vmem_of(tile // 2) <= 58 * MIB else tile // 4
+    chunks = chunks_of(colours, tile, late)
     final = len(chunks)
 
-    hbm = pl.BlockSpec(memory_space=pl.ANY)
+    hbm = pl.BlockSpec(memory_space=pltpu.HBM)
     bf16, f32, i32 = jnp.bfloat16, jnp.float32, jnp.int32
     dma = pltpu.SemaphoreType.DMA
     scratch = [pltpu.VMEM((n * tiles, h, basis), bf16) for _, _, h in chunks]
-    scratch += [pltpu.VMEM((listed + 1, tile, basis), bf16) for _ in range(colours)]
+    scratch += [pltpu.VMEM((listed + 1, h, basis), bf16) for _, _, h in units]
     scratch += [pltpu.VMEM((owned, tile, basis), bf16) for _ in range(colours)]
     scratch += [pltpu.VMEM((listed, tile, basis), bf16) for _ in range(2)]
     scratch += [pltpu.SMEM((listed,), i32) for _ in range(rows)]
     scratch += [
         pltpu.VMEM((count + 1, tile, tile), bf16),
-        pltpu.VMEM((groups, tile, GROUP * LATE), bf16),
+        pltpu.VMEM((groups, tile, GROUP * late), bf16),
         pltpu.VMEM((groups, tile, basis), bf16),
         pltpu.VMEM((colours, owned * tile), f32),
         pltpu.VMEM((tile, tile), f32),
@@ -427,24 +459,22 @@
         dma((3,)),
         dma,
         dma((colours,)),
-        dma((colours,)),
-        dma((colours, rows)),
-        dma((colours, rows)),
-        dma((colours,)),
+        dma((len(units),)),
+        dma((len(units), rows)),
+        dma((len(units), rows)),
+        dma((len(units),)),
         dma((rows,)),
         dma((rows,)),
     ]
     tile_bytes = tile * basis * 2
-    vmem = (count + 1) * tile * tile * 2 + groups * tile * (GROUP * LATE + basis) * 2
-    vmem += (n * tiles * colours + (listed + 1 + owned) * colours + 2 * listed) * tile_bytes
     out = pl.pallas_call(
-        functools.partial(fused, n, rows, colours, groups),
+        functools.partial(fused, n, rows, colours, groups, late),
         out_shape=jax.ShapeDtypeStruct((owned, tile, width), bf16),
         in_specs=[hbm] * 7,
-        out_specs=hbm,
+        out_specs=pl.BlockSpec(memory_space=pl.ANY),
         scratch_shapes=scratch,
         compiler_params=pltpu.CompilerParams(
-            collective_id=0, has_side_effects=True, vmem_limit_bytes=max(vmem + (2 << 20), 58 << 20)
+            collective_id=0, has_side_effects=True, vmem_limit_bytes=max(vmem_of(late) + 2 * MIB, 58 * MIB)
         ),
         cost_estimate=pl.CostEstimate(
             flops=2 * count * tile * tile * width,

time: 143 us -> 138 us (0.965)
  Pallas kernels: 140 us -> 135 us
    pallas_call x1, Pallas kernels: 140 us -> 135 us  [per_device(): pl.pallas_call(functools.partial(fused, n, rows, colours, groups, late),...]
where the time goes in v2:
time: 138 us
  Pallas kernels  135 us (98%)
  local copies, waits for them, and re-layouts  2.71 us (2%)
    pallas_call x1, Pallas kernels, per_device(): pl.pallas_call(functools.partial(fused, n, rows, colours, groups, late),...  135 us

profile of v2, /device:TPU:1, one launch (start us, length us, event | category | flops | bytes accessed | tf_op | source)
XLA Modules:
  0.0 137.8 jit_solution(9898778173112940492)
XLA Ops:
  0.0 135.1 %shard_map.73 = bf16[16,128,384]{2,1,0:T(8,128)(2,1)} custom-call(s32[640]{0:T(1024)} %row_ref.1, s32[640]{0:T(1024)} %col_ref.1, s32[16]{0:T(128)} %send_ref.1, bf16[640,128,128]{2,1,0:T(8,128)(2,1)} %blocks_ref.1, bf16[16,128,384]{2,1,0:T(8,128)(2,1)} %bitcast.4, f32[3,2048]{1,0:T(4,128)} %albedo_ref.1, bf16[16,128,384]{2,1,0:T(8,128)(2,1)} %bitcast.5), custom_call_target="tpu_custom_call" | custom-call | flops 8053063680 | bytes 33554432 | tf_op jit(solution)/shard_map/pallas_call | solution.py:470
  135.1 2.7 %copy.9 = bf16[2048,384]{1,0:T(8,128)(2,1)} copy(bf16[2048,384]{1,0:T(8,128)(2,1)} %bitcast.3) | data formatting | bytes 3145728

commit v3 on v2

--- a/solution.py
+++ b/solution.py
@@ -57,7 +57,6 @@
     take = iter(scratch)
     slabs = [next(take) for _ in chunks]
     arrived = [next(take) for _ in units]
-    lit = [next(take) for _ in range(colours)]
     parts = [next(take) for _ in range(2)]
     got = [next(take) for _ in range(rows)]
     (
@@ -82,7 +81,6 @@
         index_sem,
         alb_sem,
         em_sem,
-        out_sem,
         ex_send,
         ex_recv,
         ex_own,
@@ -122,15 +120,7 @@
     ]
     load = pltpu.make_async_copy(blocks_ref, blk.at[pl.ds(0, count)], blk_sem)
     load_albedo = pltpu.make_async_copy(albedo_ref, alb_in, alb_sem)
-    load_emission = [
-        pltpu.make_async_copy(emission_ref.at[:, :, pl.ds(c * basis, basis)], lit[c], em_sem.at[c]) for c in range(colours)
-    ]
-    store_out = [
-        pltpu.make_async_copy(
-            lit[c].at[:, pl.ds(o, h)], out_ref.at[:, pl.ds(o, h), pl.ds(c * basis, basis)], out_sem.at[u]
-        )
-        for u, (c, o, h) in enumerate(units)
-    ]
+    load_emission = pltpu.make_async_copy(emission_ref, out_ref, em_sem)
     pl.semaphore_wait(barrier, 2 + rows - 1)
 
     def piece(k, m, way, arriving):
@@ -198,8 +188,7 @@
             ids(d).start()
         load.start()
         load_albedo.start()
-        for copy in load_emission:
-            copy.start()
+        load_emission.start()
 
     def make_plan():
         for copy in loads:
@@ -336,16 +325,16 @@
             to_row(u, d).wait_send()
             from_row(u, d).wait_recv()
         stay(u).wait()
-        if o == 0:
-            load_emission[c].wait()
+        if u == 0:
+            load_emission.wait()
+        lanes = pl.ds(c * basis, basis)
         for t in range(owned):
             total = arrived[u][pos_s[t * rows]].astype(jnp.float32)
             for d in range(1, rows):
                 total = total + arrived[u][pos_s[t * rows + d]].astype(jnp.float32)
             scale = alb_cols[pl.ds(o, h), pl.ds(c * owned + t, 1)]
-            before = lit[c][t, pl.ds(o, h)].astype(jnp.float32)
-            lit[c][t, pl.ds(o, h)] = (total * scale + before).astype(lit[c].dtype)
-        store_out[u].start()
+            before = out_ref[t, pl.ds(o, h), lanes].astype(jnp.float32)
+            out_ref[t, pl.ds(o, h), lanes] = (total * scale + before).astype(out_ref.dtype)
 
     final = len(chunks) - 1
     steps = min(messages - 1, batches)
@@ -403,7 +392,18 @@
             piece(final, m, way, 0).wait_send()
     for u in range(colours - 1, len(units)):
         finish(u)
-    for copy in store_out:
+
+
+def write_out(from_ref, out_ref, sem):
+    pieces = sem.shape[0]
+    size = from_ref.shape[0] // pieces
+    copies = [
+        pltpu.make_async_copy(from_ref.at[pl.ds(i * size, size)], out_ref.at[pl.ds(i * size, size)], sem.at[i])
+        for i in range(pieces)
+    ]
+    for copy in copies:
+        copy.start()
+    for copy in copies:
         copy.wait()
 
 
@@ -422,7 +422,7 @@
     units = units_of(colours, tile)
 
     def vmem_of(late):
-        tall = n * tiles * colours + (listed + 1 + owned) * colours + 2 * listed + groups
+        tall = n * tiles * colours + (listed + 1) * colours + 2 * listed + groups
         return ((count + 1) * tile * tile + groups * tile * GROUP * late + tall * tile * basis) * 2
 
     late = tile // 2 if vmem_of(tile // 2) <= 58 * MIB else tile // 4
@@ -434,7 +434,6 @@
     dma = pltpu.SemaphoreType.DMA
     scratch = [pltpu.VMEM((n * tiles, h, basis), bf16) for _, _, h in chunks]
     scratch += [pltpu.VMEM((listed + 1, h, basis), bf16) for _, _, h in units]
-    scratch += [pltpu.VMEM((owned, tile, basis), bf16) for _ in range(colours)]
     scratch += [pltpu.VMEM((listed, tile, basis), bf16) for _ in range(2)]
     scratch += [pltpu.SMEM((listed,), i32) for _ in range(rows)]
     scratch += [
@@ -458,8 +457,7 @@
         dma,
         dma((3,)),
         dma,
-        dma((colours,)),
-        dma((len(units),)),
+        dma,
         dma((len(units), rows)),
         dma((len(units), rows)),
         dma((len(units),)),
@@ -469,12 +467,12 @@
     tile_bytes = tile * basis * 2
     out = pl.pallas_call(
         functools.partial(fused, n, rows, colours, groups, late),
-        out_shape=jax.ShapeDtypeStruct((owned, tile, width), bf16),
+        out_shape=pltpu.VMEM((owned, tile, width), bf16),
         in_specs=[hbm] * 7,
-        out_specs=pl.BlockSpec(memory_space=pl.ANY),
+        out_specs=pl.BlockSpec(memory_space=pltpu.VMEM),
         scratch_shapes=scratch,
         compiler_params=pltpu.CompilerParams(
-            collective_id=0, has_side_effects=True, vmem_limit_bytes=max(vmem_of(late) + 2 * MIB, 58 * MIB)
+            collective_id=0, has_side_effects=True, vmem_limit_bytes=max(vmem_of(late) + MIB, 58 * MIB)
         ),
         cost_estimate=pl.CostEstimate(
             flops=2 * count * tile * tile * width,
@@ -490,6 +488,14 @@
         albedo,
         emission.reshape(owned, tile, width),
     )
+    out = pl.pallas_call(
+        write_out,
+        out_shape=jax.ShapeDtypeStruct((owned, tile, width), bf16),
+        in_specs=[pl.BlockSpec(memory_space=pl.ANY)],
+        out_specs=pl.BlockSpec(memory_space=pl.ANY),
+        scratch_shapes=[dma((4,))],
+        compiler_params=pltpu.CompilerParams(vmem_limit_bytes=8 * MIB),
+    )(out)
     return out.reshape(owned * tile, width)
 
 

time: 138 us -> 136 us (0.986)
  local copies, waits for them, and re-layouts: 2.71 us -> 0 us
    unnamed x1 -> x0, local copies, waits for them, and re-layouts: 2.71 us -> none
where the time goes in v3:
time: 136 us
  Pallas kernels  135 us (99%)
    pallas_call x1, Pallas kernels, per_device(): pl.pallas_call(functools.partial(fused, n, rows, colours, groups, late),...  134 us

profile of v3, /device:TPU:1, one launch (start us, length us, event | category | flops | bytes accessed | tf_op | source)
XLA Modules:
  0.0 135.6 jit_solution(749345576146546559)
XLA Ops:
  0.0 134.3 %shard_map.73.from_ref = bf16[16,128,384]{2,1,0:T(8,128)(2,1)S(1)} custom-call(s32[640]{0:T(1024)} %row_ref.1, s32[640]{0:T(1024)} %col_ref.1, s32[16]{0:T(128)} %send_ref.1, bf16[640,128,128]{2,1,0:T(8,128)(2,1)} %blocks_ref.1, bf16[16,128,384]{2,1,0:T(8,128)(2,1)} %bitcast.3, f32[3,2048]{1,0:T(4,128)} %albedo_ref.1, bf16[16,128,384]{2,1,0:T(8,128)(2,1)} %bitcast.4), custom_call_target="tpu_custom_call" | custom-call | flops 8053063680 | bytes 33554432 | tf_op jit(solution)/shard_map/pallas_call | solution.py:468
  134.3 1.2 shard_map.74

commit v4 on v3

--- a/solution.py
+++ b/solution.py
@@ -381,7 +381,7 @@
     for m in range(max(messages - 2, 0), messages):
         for way in (0, 1):
             piece(final, m, way, 1).wait_recv()
-    batch = 2 * BATCH if batches % 2 == 0 else BATCH
+    batch = max(b * BATCH for b in (1, 2, 4) if batches % b == 0)
     for u in range(colours - 1, len(units)):
         c, o, h = units[u]
         operands = functools.partial(late_operands, final, o=o, h=h)

time: 136 us -> 135 us (level)
  no operation moved by 1% of the time
where the time goes in v4:
time: 135 us
  Pallas kernels  135 us (100%)
    pallas_call x1, Pallas kernels, per_device(): pl.pallas_call(functools.partial(fused, n, rows, colours, groups, late),...  133 us

profile of v4, /device:TPU:1, one launch (start us, length us, event | category | flops | bytes accessed | tf_op | source)
XLA Modules:
  0.0 134.8 jit_solution(2806313230315492036)
XLA Ops:
  0.0 133.4 %shard_map.73.from_ref = bf16[16,128,384]{2,1,0:T(8,128)(2,1)S(1)} custom-call(s32[640]{0:T(1024)} %row_ref.1, s32[640]{0:T(1024)} %col_ref.1, s32[16]{0:T(128)} %send_ref.1, bf16[640,128,128]{2,1,0:T(8,128)(2,1)} %blocks_ref.1, bf16[16,128,384]{2,1,0:T(8,128)(2,1)} %bitcast.3, f32[3,2048]{1,0:T(4,128)} %albedo_ref.1, bf16[16,128,384]{2,1,0:T(8,128)(2,1)} %bitcast.4), custom_call_target="tpu_custom_call" | custom-call | flops 8053063680 | bytes 33554432 | tf_op jit(solution)/shard_map/pallas_call | solution.py:468
  133.4 1.2 shard_map.74

commit v5 on v4

--- a/solution.py
+++ b/solution.py
@@ -30,7 +30,7 @@
 
 def units_of(colours, tile):
     whole = [(c, 0, tile) for c in range(colours - 1)]
-    return whole + [(colours - 1, 0, tile // 2), (colours - 1, tile // 2, tile // 2)]
+    return whole + [(colours - 1, 0, tile * 5 // 8), (colours - 1, tile * 5 // 8, tile * 3 // 8)]
 
 
 def fused(

time: 135 us -> 135 us (level)
  no operation moved by 1% of the time
where the time goes in v5:
time: 135 us
  Pallas kernels  134 us (99%)
    pallas_call x1, Pallas kernels, per_device(): pl.pallas_call(functools.partial(fused, n, rows, colours, groups, late),...  133 us

profile of v5, /device:TPU:1, one launch (start us, length us, event | category | flops | bytes accessed | tf_op | source)
XLA Modules:
  0.0 134.6 jit_solution(4554715861009638851)
XLA Ops:
  0.0 133.2 %shard_map.73.from_ref = bf16[16,128,384]{2,1,0:T(8,128)(2,1)S(1)} custom-call(s32[640]{0:T(1024)} %row_ref.1, s32[640]{0:T(1024)} %col_ref.1, s32[16]{0:T(128)} %send_ref.1, bf16[640,128,128]{2,1,0:T(8,128)(2,1)} %blocks_ref.1, bf16[16,128,384]{2,1,0:T(8,128)(2,1)} %bitcast.3, f32[3,2048]{1,0:T(4,128)} %albedo_ref.1, bf16[16,128,384]{2,1,0:T(8,128)(2,1)} %bitcast.4), custom_call_target="tpu_custom_call" | custom-call | flops 8053063680 | bytes 33554432 | tf_op jit(solution)/shard_map/pallas_call | solution.py:468
  133.2 1.2 shard_map.74

commit v6 on v4

--- a/solution.py
+++ b/solution.py
@@ -304,7 +304,7 @@
         return lax.fori_loop(low, high, one, running)
 
     def collect(c, o, h, add, u):
-        for d in list(range(rows // 2, rows)) + list(range(rows // 2)):
+        for d in list(range(rows // 2, rows)) + list(range(1, rows // 2)) + [0]:
             target = (prow + d) % rows
             for j in range(per):
                 s = target * per + j

time: 135 us -> 135 us (level)
  no operation moved by 1% of the time
where the time goes in v6:
time: 135 us
  Pallas kernels  135 us (100%)
    pallas_call x1, Pallas kernels, per_device(): pl.pallas_call(functools.partial(fused, n, rows, colours, groups, late),...  133 us

profile of v6, /device:TPU:1, one launch (start us, length us, event | category | flops | bytes accessed | tf_op | source)
XLA Modules:
  0.0 134.8 jit_solution(3584383652850480270)
XLA Ops:
  0.0 133.4 %shard_map.73.from_ref = bf16[16,128,384]{2,1,0:T(8,128)(2,1)S(1)} custom-call(s32[640]{0:T(1024)} %row_ref.1, s32[640]{0:T(1024)} %col_ref.1, s32[16]{0:T(128)} %send_ref.1, bf16[640,128,128]{2,1,0:T(8,128)(2,1)} %blocks_ref.1, bf16[16,128,384]{2,1,0:T(8,128)(2,1)} %bitcast.3, f32[3,2048]{1,0:T(4,128)} %albedo_ref.1, bf16[16,128,384]{2,1,0:T(8,128)(2,1)} %bitcast.4), custom_call_target="tpu_custom_call" | custom-call | flops 8053063680 | bytes 33554432 | tf_op jit(solution)/shard_map/pallas_call | solution.py:468
  133.4 1.2 shard_map.74
